TPU v7x, 512 devices: a whole 4x8x8 slice. The times are simulated.
512 devices in a mesh: rows: 64 (over z, y), feat: 8 (over x, core).
Axes of the slice: x: 4, y: 8, z: 8, core: 2. Of those that a mesh axis runs over, the one named last changes fastest.
Arguments:
- predictions: bfloat16 [98304, 4096], P('rows', 'feat'), may hold values from -9 to 9
- targets: bfloat16 [98304, 4096], P('rows', 'feat'), may hold values from 0 to 1
- sketch_matrix: bfloat16 [32, 4096], P(None, 'feat'), may hold values from -0.0048828125 to 0.0048828125
- bin_codes: int32 [256, 98304], P('feat', 'rows'), may hold values from 0 to 255
- row_node: int32 [98304], P('rows'), may hold values from 0 to 3
- smaller: int32 [4], replicated, may hold values from 0 to 1, as said below
- split_feature: int32 [4], replicated, may hold values from 0 to 255
- split_bin: int32 [4], replicated, may hold values from 64 to 191
Outputs:
- new_predictions: bfloat16 [98304, 4096], P('rows', 'feat')
- histograms: float32 [256, 16384], P('rows', 'feat')
Inputs may be any that keep to these rules, and one draw needn't show every extreme that they name: Of the nodes 2 p and 2 p + 1 exactly one has smaller equal to 1.
All inputs are finite; a program needn't handle non-finite values.
Results may differ from a plain program's by a relative error of at most 0.0034.
Values sent between devices are 32-bit elements; how exact they have to be, the bound alone decides.
A program may use at most 64 MiB of HBM per device.

v0:
```python
import math
import jax
import jax.numpy as jnp
from jax import lax
from jax.sharding import PartitionSpec as P

BINS = 256
DAMPING = 1.0
SHRINKAGE = 0.5


def per_device(
    predictions, targets, sketch_matrix, bin_codes, row_node, smaller, split_feature, split_bin
):
    row_count = predictions.shape[0]
    feat_dev = bin_codes.shape[0]
    node_total = smaller.shape[0]
    slot_total = node_total // 2
    leaf_total = 2 * node_total
    column_dev = lax.axis_index("feat")
    logits = predictions.astype(jnp.float32)
    probability = jax.nn.sigmoid(logits)
    gradient = (probability - targets.astype(jnp.float32)).astype(jnp.bfloat16)
    hessian = (probability * (1.0 - probability)).astype(jnp.bfloat16)
    partial_value = lax.dot_general(
        gradient, sketch_matrix, (((1,), (1,)), ((), ())), preferred_element_type=jnp.float32
    )
    node_hot = (row_node[:, None] == jnp.arange(node_total, dtype=jnp.int32)[None, :]).astype(
        jnp.int32
    )
    feat_row = jnp.sum(node_hot * split_feature[None, :], axis=1)
    thresh_row = jnp.sum(node_hot * split_bin[None, :], axis=1)
    small_row = jnp.sum(node_hot * smaller[None, :], axis=1)
    local_feat = feat_row - column_dev * feat_dev
    selector = jnp.arange(feat_dev, dtype=jnp.int32)[:, None] == local_feat[None, :]
    code_at = jnp.sum(jnp.where(selector, bin_codes, 0), axis=0)
    owned = jnp.any(selector, axis=0)
    right_part = jnp.where(owned & (code_at > thresh_row), 1.0, 0.0).astype(jnp.float32)
    sketch, right_side = lax.psum((partial_value, right_part), "feat")
    leaf_id = 2 * row_node + (right_side > 0.5).astype(jnp.int32)
    slot_mask = ((row_node // 2)[:, None] == jnp.arange(slot_total, dtype=jnp.int32)[None, :]) & (
        small_row == 1
    )[:, None]
    weighted = (
        (slot_mask.astype(jnp.float32)[:, :, None] * sketch[:, None, :])
        .reshape(row_count, -1)
        .astype(jnp.bfloat16)
    )
    width = weighted.shape[1]
    group_size = math.gcd(feat_dev, 8)
    grouped = bin_codes.reshape(feat_dev // group_size, group_size, row_count)
    bin_ids = jnp.arange(BINS, dtype=jnp.int32)

    def one_group(codes_group):
        one_hot = (codes_group[:, None, :] == bin_ids[None, :, None]).astype(jnp.bfloat16)
        return lax.dot_general(
            one_hot, weighted, (((2,), (0,)), ((), ())), preferred_element_type=jnp.float32
        )

    stacked = lax.map(one_group, grouped).reshape(feat_dev, BINS, width)
    histograms = lax.psum_scatter(
        stacked.transpose(1, 0, 2).reshape(BINS, feat_dev * width),
        "rows",
        scatter_dimension=0,
        tiled=True,
    )
    leaf_match = jnp.arange(leaf_total, dtype=jnp.int32)[:, None] == leaf_id[None, :]
    leaf_hot = leaf_match.astype(jnp.bfloat16)
    grad_sum = jnp.dot(leaf_hot, gradient, preferred_element_type=jnp.float32)
    hess_sum = jnp.dot(leaf_hot, hessian, preferred_element_type=jnp.float32)
    grad_own, hess_own = (
        lax.psum_scatter(grad_sum, "rows", scatter_dimension=1, tiled=True),
        lax.psum_scatter(hess_sum, "rows", scatter_dimension=1, tiled=True),
    )
    owned_values = -grad_own / (hess_own + DAMPING)
    values = lax.all_gather(owned_values, "rows", axis=1, tiled=True)
    update = jnp.dot(leaf_match.T.astype(jnp.float32), values, precision=lax.Precision.HIGHEST)
    new_predictions = (logits + SHRINKAGE * update).astype(jnp.bfloat16)
    return (new_predictions, histograms)


def solution(mesh):
    placed = (
        P("rows", "feat"),
        P("rows", "feat"),
        P(None, "feat"),
        P("feat", "rows"),
        P("rows"),
        P(),
        P(),
        P(),
    )
    return jax.shard_map(
        per_device,
        mesh=mesh,
        in_specs=placed,
        out_specs=(P("rows", "feat"), P("rows", "feat")),
        check_vma=False,
    )
```

profile of v0, /device:TPU:8, one launch (start us, length us, event | category | flops | bytes accessed | tf_op | source)
XLA Modules:
  0.0 445.8 jit_solution(7354228785645584075)
XLA Ops:
  7.3 2.9 subtract_convert_fusion
  10.2 1.2 fusion.28
  11.5 0.1 select_reduce_fusion.1
  11.8 14.9 %psum.14 = f32[1536]{0:T(1024)S(1)} all-reduce(f32[1536]{0:T(1024)S(1)} %and_select_fusion), channel_id=1, replica_groups=mesh['rows'=64,'feat'=8] {'feat'}, use_global_device_ids=true, to_apply=%region_4.5 | all-reduce | flops 1536 | bytes 12288 | tf_op jit(solution)/shard_map/psum | solution.py:39
  26.7 59.8 %all-reduce.7.cloned.1.call-done = f32[1536,32]{0,1:T(8,128)} async-done(((f32[1536,32]{0,1:T(8,128)}), f32[1536,32]{0,1:T(8,128)}) %all-reduce.7.cloned.1.call-update) | async-done | bytes 196624 | tf_op jit(solution)/shard_map/psum | solution.py:39
  86.5 16.0 %while.11 = (s32[]{:T(128)}, f32[4,8,256,64]{2,3,1,0:T(8,128)}, s32[4,8,1536]{2,1,0:T(8,128)S(1)}, f32[1536,32]{0,1:T(8,128)}, f32[1536,2]{0,1:T(2,128)S(1)}, /*index=5*/s32[]{:T(128)}) while((s32[]{:T(128)}, f32[4,8,256,64]{2,3,1,0:T(8,128)}, s32[4,8,1536]{2,1,0:T(8,128)S(1)}, f32[1536,32]{0,1:T(8,128)}, ...), condition=%wide.region_10.11_spmd.clone, body=%wide.region_9.10_spmd.clone.sunk | while | flops 405995520 | bytes 1274441 | solution.py:60
  86.5 1.0 multiply_convert_fusion.2
  87.5 3.0 fusion.37
  90.5 1.0 multiply_convert_fusion.2
  91.5 3.1 fusion.37
  94.5 1.0 multiply_convert_fusion.2
  95.5 3.0 fusion.37
  98.5 1.0 multiply_convert_fusion.2
  99.5 3.1 fusion.37
  102.6 1.4 dynamic-slice
  104.6 0.3 fusion.19
  104.9 0.9 fusion.13
  105.9 275.4 %all-reduce.3 = (f32[8,512]{1,0:T(8,128)S(1)}, f32[8,512]{1,0:T(8,128)S(1)}) all-reduce(f32[8,512]{1,0:T(8,128)S(1)} %fusion.13, f32[8,512]{1,0:T(8,128)S(1)} %fusion.19), channel_id=3, replica_groups=mesh['rows'=64,'feat'=8] {'rows'}, use_global_device_ids=true, to_apply=%region_6.7.clone | all-reduce | flops 8192 | bytes 65536
  381.3 0.1 fusion.26
  381.4 0.1 copy.14
  382.1 51.7 %all_gather.3 = f32[8,512]{0,1:T(8,128)S(1)} all-gather(f32[8,8]{0,1:T(8,128)S(1)} %copy.14), channel_id=1, replica_groups=mesh['rows'=64,'feat'=8] {'rows'}, dimensions={1}, use_global_device_ids=true | all-gather | bytes 16640 | tf_op jit(solution)/shard_map/all_gather | solution.py:76
  433.8 2.7 fusion.12
  436.5 1.6 constant_dynamic-slice_fusion
  438.1 0.9 copy.15
  (31 shorter events, 0.3 us)
Async XLA Ops:
  7.2 3.0 copy-start
  7.2 4.3 copy-start.3
  7.2 4.3 copy-start.4
  7.2 4.3 copy-start.5
  7.2 4.3 copy-start.6
  7.2 79.3 %all-reduce.7.cloned.1.call-start = ((), (), s32[]{:S(2)}) async-start(), calls=%async_computation | async-start | bytes 393216 | tf_op jit(solution)/shard_map/psum | solution.py:39
  10.2 1.6 copy-start.2
  11.5 425.1 %all-reduce.9.cloned.1.call-start = ((), (), s32[]{:S(2)}) async-start(), calls=%async_computation.1 | async-start | bytes 4194304
  102.5 2.4 copy-start.1
Sparse Core Ops, SparseCore 0:
  11.6 74.8 all-reduce.6
  102.7 162.4 all-reduce.8
where the time goes:
time: 446 us
  blocking collectives  342 us (77%)
  waiting for transfers between devices  59.8 us (13%)
  matrix products  17.4 us (4%)
  between operations  15.5 us (3%)
  other arithmetic  7.02 us (2%)
    unnamed x1, blocking collectives  275 us
    psum x1, waiting for transfers between devices, per_device(): sketch, right_side = lax.psum((partial_value, right_part), 'feat')  59.8 us
    all_gather x1, blocking collectives, per_device(): values = lax.all_gather(owned_values, 'rows', axis=1, tiled=True)  51.7 us
    psum x1, blocking collectives, per_device(): sketch, right_side = lax.psum((partial_value, right_part), 'feat')  14.9 us
    dot_general x4, matrix products, one_group(): lax.dot_general(one_hot, weighted, (((2,), (0,)), ((), ())), preferred_el...  12.2 us
  transfers between devices with their start and end apart: 2, of which 1 were waited for; matrix products, arithmetic and copies ran while one was open for 1% of the time, Pallas kernels for 0%

commit v1 on v0

--- a/solution.py
+++ b/solution.py
@@ -73,7 +73,9 @@
         lax.psum_scatter(hess_sum, "rows", scatter_dimension=1, tiled=True),
     )
     owned_values = -grad_own / (hess_own + DAMPING)
-    values = lax.all_gather(owned_values, "rows", axis=1, tiled=True)
+    values = jnp.concatenate(
+        lax.all_to_all(jnp.stack([owned_values] * lax.axis_size("rows")), "rows", 0, 0), axis=1
+    )
     update = jnp.dot(leaf_match.T.astype(jnp.float32), values, precision=lax.Precision.HIGHEST)
     new_predictions = (logits + SHRINKAGE * update).astype(jnp.bfloat16)
     return (new_predictions, histograms)

time: 446 us -> 418 us (0.937)
  blocking collectives: 342 us -> 291 us
  waiting for transfers between devices: 59.8 us -> 72.2 us
  starting transfers between devices: 0.08 us -> 9.97 us
    all_gather x1 -> x0, blocking collectives: 51.7 us -> none  [per_device(): values = lax.all_gather(owned_values, 'rows', axis=1, tiled=True)]
    all_to_all x0 -> x1, waiting for transfers between devices: none -> 12.4 us  [per_device(): lax.all_to_all(jnp.stack([owned_values] * lax.axis_size('rows')), 'rows',...]
    all_to_all x0 -> x1, starting transfers between devices: none -> 9.89 us  [per_device(): lax.all_to_all(jnp.stack([owned_values] * lax.axis_size('rows')), 'rows',...]
  transfers between devices with their start and end apart: 2 -> 3, of which waited for: 1 -> 2; matrix products, arithmetic and copies ran while one was open for 1% -> 2% of each run, Pallas kernels for 0% -> 0%
where the time goes in v1:
time: 418 us
  blocking collectives  291 us (70%)
  waiting for transfers between devices  72.2 us (17%)
  matrix products  17.4 us (4%)
  between operations  15.5 us (4%)
  starting transfers between devices  9.97 us (2%)
  other arithmetic  7.02 us (2%)
  local copies, waits for them, and re-layouts  4.88 us (1%)
    unnamed x1, blocking collectives  276 us
    psum x1, waiting for transfers between devices, per_device(): sketch, right_side = lax.psum((partial_value, right_part), 'feat')  59.8 us
    psum x1, blocking collectives, per_device(): sketch, right_side = lax.psum((partial_value, right_part), 'feat')  14.9 us
    all_to_all x1, waiting for transfers between devices, per_device(): lax.all_to_all(jnp.stack([owned_values] * lax.axis_size('rows')), 'rows',...  12.4 us
    dot_general x4, matrix products, one_group(): lax.dot_general(one_hot, weighted, (((2,), (0,)), ((), ())), preferred_el...  12.2 us
    all_to_all x1, starting transfers between devices, per_device(): lax.all_to_all(jnp.stack([owned_values] * lax.axis_size('rows')), 'rows',...  9.89 us
  transfers between devices with their start and end apart: 3, of which 2 were waited for; matrix products, arithmetic and copies ran while one was open for 2% of the time, Pallas kernels for 0%

profile of v1, /device:TPU:8, one launch (start us, length us, event | category | flops | bytes accessed | tf_op | source)
XLA Modules:
  0.0 417.6 jit_solution(4329062136944884956)
XLA Ops:
  7.3 2.9 subtract_convert_fusion
  10.2 1.2 fusion.26
  11.8 14.9 %psum.14 = f32[1536]{0:T(1024)S(1)} all-reduce(f32[1536]{0:T(1024)S(1)} %and_select_fusion), channel_id=1, replica_groups=mesh['rows'=64,'feat'=8] {'feat'}, use_global_device_ids=true, to_apply=%region_4.5 | all-reduce | flops 1536 | bytes 12288 | tf_op jit(solution)/shard_map/psum | solution.py:39
  26.7 59.8 %all-reduce.7.cloned.1.call-done = f32[1536,32]{0,1:T(8,128)} async-done(((f32[1536,32]{0,1:T(8,128)}), f32[1536,32]{0,1:T(8,128)}) %all-reduce.7.cloned.1.call-update) | async-done | bytes 196624 | tf_op jit(solution)/shard_map/psum | solution.py:39
  86.5 16.0 %while.11 = (s32[]{:T(128)}, f32[4,8,256,64]{2,3,1,0:T(8,128)}, s32[4,8,1536]{2,1,0:T(8,128)S(1)}, f32[1536,32]{0,1:T(8,128)}, f32[1536,2]{0,1:T(2,128)S(1)}, /*index=5*/s32[]{:T(128)}) while((s32[]{:T(128)}, f32[4,8,256,64]{2,3,1,0:T(8,128)}, s32[4,8,1536]{2,1,0:T(8,128)S(1)}, f32[1536,32]{0,1:T(8,128)}, ...), condition=%wide.region_10.11_spmd.clone, body=%wide.region_9.10_spmd.clone.sunk | while | flops 405995520 | bytes 1274441 | solution.py:60
  86.5 1.0 multiply_convert_fusion.2
  87.5 3.0 fusion.35
  90.5 1.0 multiply_convert_fusion.2
  91.5 3.1 fusion.35
  94.5 1.0 multiply_convert_fusion.2
  95.5 3.0 fusion.35
  98.5 1.0 multiply_convert_fusion.2
  99.5 3.1 fusion.35
  102.6 1.4 dynamic-slice
  104.6 0.3 fusion.18
  104.9 0.9 fusion.13
  105.9 275.7 %all-reduce.3 = (f32[8,512]{1,0:T(8,128)S(1)}, f32[8,512]{1,0:T(8,128)S(1)}) all-reduce(f32[8,512]{1,0:T(8,128)S(1)} %fusion.13, f32[8,512]{1,0:T(8,128)S(1)} %fusion.18), channel_id=3, replica_groups=mesh['rows'=64,'feat'=8] {'rows'}, use_global_device_ids=true, to_apply=%region_6.7.clone | all-reduce | flops 8192 | bytes 65536
  381.6 0.7 stack.2
  382.4 9.9 %all-to-all-start = ((f32[64,8,8]{2,1,0:T(8,128)}), f32[64,8,8]{2,1,0:T(8,128)S(1)}, u32[]{:S(2)}, u32[]{:S(2)}) async-start(f32[64,8,8]{2,1,0:T(8,128)} %stack.2), calls=%async_computation | async-start | bytes 524288 | tf_op jit(solution)/shard_map/all_to_all | solution.py:77
  392.9 12.4 %all-to-all-done = f32[64,8,8]{2,1,0:T(8,128)S(1)} async-done(((f32[64,8,8]{2,1,0:T(8,128)}), f32[64,8,8]{2,1,0:T(8,128)S(1)}, u32[]{:S(2)}, u32[]{:S(2)}) %all-to-all-start) | async-done | bytes 16416 | tf_op jit(solution)/shard_map/all_to_all | solution.py:77
  405.4 0.2 reshape.79
  405.5 2.7 fusion.12
  408.2 1.6 constant_dynamic-slice_fusion
  409.8 0.9 copy.15
  (34 shorter events, 0.5 us)
Async XLA Ops:
  7.2 3.0 copy-start
  7.2 4.3 %copy-start.3 = (s32[1536]{0:T(1024)S(1)}, s32[1536]{0:T(1024)}, u32[]{:S(2)}) copy-start(s32[1536]{0:T(1024)} %param.14) | copy-start | bytes 18436
  7.2 4.3 %copy-start.4 = (s32[4]{0:T(128)S(1)}, s32[4]{0:T(128)}, u32[]{:S(2)}) copy-start(s32[4]{0:T(128)} %param.15) | copy-start | bytes 52
  7.2 4.3 %copy-start.5 = (s32[4]{0:T(128)S(1)}, s32[4]{0:T(128)}, u32[]{:S(2)}) copy-start(s32[4]{0:T(128)} %param.16) | copy-start | bytes 52
  7.2 4.3 %copy-start.6 = (s32[4]{0:T(128)S(1)}, s32[4]{0:T(128)}, u32[]{:S(2)}) copy-start(s32[4]{0:T(128)} %param.17) | copy-start | bytes 52
  7.2 79.3 %all-reduce.7.cloned.1.call-start = ((), (), s32[]{:S(2)}) async-start(), calls=%async_computation.1 | async-start | bytes 393216 | tf_op jit(solution)/shard_map/psum | solution.py:39
  10.2 1.6 copy-start.2
  11.5 396.8 %all-reduce.9.cloned.1.call-start = ((), (), s32[]{:S(2)}) async-start(), calls=%async_computation.2 | async-start | bytes 4194304
  102.5 2.4 copy-start.1
  382.4 23.0 %all-to-all-start = ((f32[64,8,8]{2,1,0:T(8,128)}), f32[64,8,8]{2,1,0:T(8,128)S(1)}, u32[]{:S(2)}, u32[]{:S(2)}) async-start(f32[64,8,8]{2,1,0:T(8,128)} %stack.2), calls=%async_computation | async-start | bytes 524288 | tf_op jit(solution)/shard_map/all_to_all | solution.py:77
Sparse Core Ops, SparseCore 0:
  11.6 74.8 all-reduce.6
  102.7 162.4 all-reduce.8
